TPU v7x, 32 devices: a whole 2x2x4 slice. The times are simulated.
32 devices in a mesh: ctx: 8 (over z, x), wsh: 4 (over y, core).
Axes of the slice: x: 2, y: 2, z: 4, core: 2. Of those that a mesh axis runs over, the one named last changes fastest.
Arguments:
- tokens: bfloat16 [16, 2048, 768], P('wsh', 'ctx'), may hold values from -6 to 6
- doc_begin: int32 [16, 8], P('wsh', 'ctx'), may hold values from 0 to 4, as said below
- gain_attn: bfloat16 [768], P('wsh'), may hold values from 0.099609375 to 1.8984375
- w_qkv: bfloat16 [768, 2304], P('wsh'), may hold values from -0.21875 to 0.21875
- w_att_out: bfloat16 [768, 768], P('wsh'), may hold values from -1.75 to 1.75
- gain_mlp: bfloat16 [768], P('wsh'), may hold values from 0.099609375 to 1.8984375
- w_in: bfloat16 [768, 2304], P('wsh'), may hold values from -0.21875 to 0.21875
- w_down: bfloat16 [1152, 768], P('wsh'), may hold values from -0.1875 to 0.1875
- cotangent: bfloat16 [16, 2048, 768], P('wsh', 'ctx'), may hold values from -6 to 6
Outputs:
- output: bfloat16 [16, 2048, 768], P('wsh', 'ctx')
- grad_tokens: bfloat16 [16, 2048, 768], P('wsh', 'ctx')
- grad_gain_attn: float32 [768], P('wsh')
- grad_w_qkv: float32 [768, 2304], P('wsh')
- grad_w_att_out: float32 [768, 768], P('wsh')
- grad_gain_mlp: float32 [768], P('wsh')
- grad_w_in: float32 [768, 2304], P('wsh')
- grad_w_down: float32 [1152, 768], P('wsh')
Inputs may be any that keep to these rules, and one draw needn't show every extreme that they name: `doc_begin`: never above the block's own index along the pack; every document begins at a block whose index is a multiple of 4 and holds 1024 tokens or more; of the 4 packs that share an index of wsh, one is a single document.
All inputs are finite; a program needn't handle non-finite values.
Results may differ from a plain program's by a relative error of at most 0.015.
Values may be sent and summed in bfloat16 or wider, within the bound.
No kernel may reach another device: no remote copies, remote signals or barrier semaphores. Data moves between devices by JAX's collectives and lax.ppermute only.
A program may use at most 192 MiB of HBM per device.

v0:
```python
import jax
import jax.numpy as jnp
from jax import lax
from jax.sharding import PartitionSpec as P

HEAD = 64
FF = 1152
HALF = 64


EPS = 1e-05
THETA = 10000.0
MASKED = -1e30


def extended(value, sides, width):
    for axis, dim in sides:
        peers, length = (lax.axis_size(axis), value.shape[dim])
        up = [(i, (i + 1) % peers) for i in range(peers - 1)]
        down = [(j, i) for i, j in up]
        last = lax.slice_in_dim(value, length - width, length, axis=dim)
        leading = lax.slice_in_dim(value, 0, width, axis=dim)
        before = lax.ppermute(last, axis, up)
        after = lax.ppermute(leading, axis, down)
        value = jnp.concatenate([before, value, after], axis=dim)
    return value


def passed_along(value, axis, by):
    peers = lax.axis_size(axis)
    pairs = [(i, i + by) for i in range(peers) if 0 <= i + by < peers]
    return lax.ppermute(value, axis, pairs)


def normalize(values, gain):
    average = jnp.mean(values, axis=-1, keepdims=True)
    centred = values - average
    inverse = lax.rsqrt(jnp.mean(centred * centred, axis=-1, keepdims=True) + EPS)
    normal = centred * inverse
    return (normal * gain, normal, inverse)


def norm_back(incoming, normal, inverse, gain):
    scaled = incoming * gain
    inner = (
        scaled
        - jnp.mean(scaled, axis=-1, keepdims=True)
        - normal * jnp.mean(scaled * normal, axis=-1, keepdims=True)
    )
    return (inverse * inner, jnp.sum(incoming * normal, axis=0))


def rotary_tables(positions):
    half_size = HEAD // 2
    freqs = jnp.power(THETA, -jnp.arange(half_size, dtype=jnp.float32) * (2.0 / HEAD))
    angles = positions[:, None] * freqs[None, :]
    cosine = jnp.concatenate([jnp.cos(angles), jnp.cos(angles)], axis=-1)[:, None, :]
    sine_tab = jnp.concatenate([jnp.sin(angles), jnp.sin(angles)], axis=-1)[:, None, :]
    return (cosine, sine_tab)


def rotate(values, cosine, sine_tab):
    half_size = values.shape[-1] // 2
    turned = jnp.concatenate([-values[..., half_size:], values[..., :half_size]], axis=-1)
    return values * cosine + turned * sine_tab


def rotate_back(incoming, cosine, sine_tab):
    half_size = incoming.shape[-1] // 2
    sined = incoming * sine_tab
    turned = jnp.concatenate([sined[..., half_size:], -sined[..., :half_size]], axis=-1)
    return incoming * cosine + turned


def contract_rows(left, right):
    return lax.dot_general(
        left, right, (((0,), (0,)), ((), ())), preferred_element_type=jnp.float32
    )


def against(left, right):
    return lax.dot_general(
        left, right, (((1,), (1,)), ((), ())), preferred_element_type=jnp.float32
    )


def gelu_exact(argument):
    return jax.nn.gelu(argument, approximate=False)


def per_device(tokens, doc_begin, gain_attn, w_qkv, w_att_out, gain_mlp, w_in, w_down, cotangent):
    packs, block_len, model_width = tokens.shape
    row_count = packs * block_len
    head_count = model_width // HEAD
    key_span = block_len + 2 * HALF
    score_scale = HEAD ** (-0.5)
    gain_one, qkv_full, out_full, gain_two, in_full, down_full = (
        lax.all_gather(gain_attn, "wsh", axis=0, tiled=True),
        lax.all_gather(w_qkv, "wsh", axis=0, tiled=True),
        lax.all_gather(w_att_out, "wsh", axis=0, tiled=True),
        lax.all_gather(gain_mlp, "wsh", axis=0, tiled=True),
        lax.all_gather(w_in, "wsh", axis=0, tiled=True),
        lax.all_gather(w_down, "wsh", axis=0, tiled=True),
    )
    gain_one = gain_one.astype(jnp.float32)
    gain_two = gain_two.astype(jnp.float32)
    inputs = tokens.reshape(row_count, model_width).astype(jnp.float32)
    normed, normal_one, inverse_one = normalize(inputs, gain_one)
    first_in = normed.astype(jnp.bfloat16)
    projected = jnp.dot(first_in, qkv_full, preferred_element_type=jnp.float32)
    projected = projected.reshape(packs, block_len, 3, head_count, HEAD)
    positions = (lax.axis_index("ctx") * block_len + jnp.arange(block_len, dtype=jnp.int32)).astype(
        jnp.float32
    )
    cosine, sine_tab = rotary_tables(positions)
    queries = rotate(projected[:, :, 0], cosine, sine_tab).astype(jnp.bfloat16)
    keys_own = rotate(projected[:, :, 1], cosine, sine_tab).astype(jnp.bfloat16)
    values_own = projected[:, :, 2].astype(jnp.bfloat16)
    own_pair = jnp.concatenate(
        [
            keys_own.reshape(packs, block_len, model_width),
            values_own.reshape(packs, block_len, model_width),
        ],
        axis=-1,
    )
    doc_value = jnp.broadcast_to((doc_begin + 1).astype(jnp.bfloat16), (packs, block_len))
    pair_ext, doc_ext = (
        extended(own_pair, (("ctx", 1),), HALF),
        extended(doc_value, (("ctx", 1),), HALF),
    )
    keys_ext = pair_ext[:, :, :model_width].reshape(packs, key_span, head_count, HEAD)
    values_ext = pair_ext[:, :, model_width:].reshape(packs, key_span, head_count, HEAD)
    offsets = jnp.arange(key_span)[None, :] - HALF - jnp.arange(block_len)[:, None]
    allowed = (jnp.abs(offsets) <= HALF)[None, :, :] & (
        doc_ext[:, None, :] == doc_value[:, :, None]
    )

    def scores_of():
        raw = (
            jnp.einsum("lqhd,lkhd->lhqk", queries, keys_ext, preferred_element_type=jnp.float32)
            * score_scale
        )
        return jnp.where(allowed[:, None], raw, MASKED)

    scores = scores_of()
    row_max = jnp.max(scores, axis=-1, keepdims=True)
    powers = jnp.exp(scores - row_max)
    row_total = jnp.sum(powers, axis=-1, keepdims=True)
    logsum = row_max + jnp.log(row_total)
    probs = (powers / row_total).astype(jnp.bfloat16)
    attended = jnp.einsum("lhqk,lkhd->lqhd", probs, values_ext, preferred_element_type=jnp.float32)
    attn_mixed = attended.reshape(row_count, model_width).astype(jnp.bfloat16)
    middle = inputs + jnp.dot(attn_mixed, out_full, preferred_element_type=jnp.float32)
    normed_two, normal_two, inverse_two = normalize(middle, gain_two)
    second_in = normed_two.astype(jnp.bfloat16)
    gate_up = jnp.dot(second_in, in_full, preferred_element_type=jnp.float32)
    gate_in = gate_up[:, :FF]
    up_part = gate_up[:, FF:]
    activated, gelu_pull = jax.vjp(gelu_exact, gate_in)
    hidden = (activated * up_part).astype(jnp.bfloat16)
    result = middle + jnp.dot(hidden, down_full, preferred_element_type=jnp.float32)
    output = result.reshape(packs, block_len, model_width).astype(jnp.bfloat16)
    upstream = cotangent.reshape(row_count, model_width)
    grad_down = contract_rows(hidden, upstream)
    grad_hidden = against(upstream, down_full)
    grad_gate_in = gelu_pull(grad_hidden * up_part)[0]
    grad_gate_up = jnp.concatenate([grad_gate_in, grad_hidden * activated], axis=-1).astype(
        jnp.bfloat16
    )
    grad_in = contract_rows(second_in, grad_gate_up)
    grad_second = against(grad_gate_up, in_full)
    grad_middle_norm, grad_gain_two = norm_back(grad_second, normal_two, inverse_two, gain_two)
    grad_middle = upstream.astype(jnp.float32) + grad_middle_norm
    middle_low = grad_middle.astype(jnp.bfloat16)
    grad_out_w = contract_rows(attn_mixed, middle_low)
    grad_mixed = (
        against(middle_low, out_full)
        .astype(jnp.bfloat16)
        .reshape(packs, block_len, head_count, HEAD)
    )
    probs_back = jnp.exp(scores_of() - logsum)
    grad_probs = jnp.einsum(
        "lqhd,lkhd->lhqk", grad_mixed, values_ext, preferred_element_type=jnp.float32
    )
    row_inner = jnp.sum(grad_probs * probs_back, axis=-1, keepdims=True)
    grad_scores = (probs_back * (grad_probs - row_inner)).astype(jnp.bfloat16)
    grad_queries = (
        jnp.einsum("lhqk,lkhd->lqhd", grad_scores, keys_ext, preferred_element_type=jnp.float32)
        * score_scale
    )
    grad_keys_ext = (
        jnp.einsum("lhqk,lqhd->lkhd", grad_scores, queries, preferred_element_type=jnp.float32)
        * score_scale
    )
    grad_values_ext = jnp.einsum(
        "lhqk,lqhd->lkhd",
        probs_back.astype(jnp.bfloat16),
        grad_mixed,
        preferred_element_type=jnp.float32,
    )
    grad_pair = jnp.concatenate(
        [
            grad_keys_ext.reshape(packs, key_span, model_width),
            grad_values_ext.reshape(packs, key_span, model_width),
        ],
        axis=-1,
    )
    from_right = passed_along(grad_pair[:, :HALF], "ctx", -1)
    from_left = passed_along(grad_pair[:, HALF + block_len :], "ctx", 1)
    grad_own = grad_pair[:, HALF : HALF + block_len]
    grad_own = grad_own.at[:, block_len - HALF :].add(from_right)
    grad_own = grad_own.at[:, :HALF].add(from_left)
    grad_keys = grad_own[:, :, :model_width].reshape(packs, block_len, head_count, HEAD)
    grad_query_pre = rotate_back(grad_queries, cosine, sine_tab).reshape(
        packs, block_len, model_width
    )
    grad_keys_pre = rotate_back(grad_keys, cosine, sine_tab).reshape(packs, block_len, model_width)
    grad_projected = jnp.concatenate(
        [grad_query_pre, grad_keys_pre, grad_own[:, :, model_width:]], axis=-1
    )
    grad_projected = grad_projected.reshape(row_count, 3 * model_width).astype(jnp.bfloat16)
    grad_qkv = contract_rows(first_in, grad_projected)
    grad_first = against(grad_projected, qkv_full)
    grad_input_norm, grad_gain_one = norm_back(grad_first, normal_one, inverse_one, gain_one)
    grad_tokens = (
        (grad_middle + grad_input_norm).reshape(packs, block_len, model_width).astype(jnp.bfloat16)
    )
    partials = (grad_gain_one, grad_qkv, grad_out_w, grad_gain_two, grad_in, grad_down)
    summed = lax.psum(
        (partials[0], partials[1], partials[2], partials[3], partials[4], partials[5]),
        ("ctx", "wsh"),
    )
    shard_index = lax.axis_index("wsh")
    group_size = lax.axis_size("wsh")
    weight_grads = tuple(
        (
            lax.dynamic_slice_in_dim(
                summed_full,
                shard_index * (summed_full.shape[0] // group_size),
                summed_full.shape[0] // group_size,
                0,
            )
            for summed_full in summed
        )
    )
    return (
        output,
        grad_tokens,
        weight_grads[0],
        weight_grads[1],
        weight_grads[2],
        weight_grads[3],
        weight_grads[4],
        weight_grads[5],
    )


def solution(mesh):
    return jax.shard_map(
        per_device,
        mesh=mesh,
        in_specs=(
            P("wsh", "ctx", None),
            P("wsh", "ctx"),
            P("wsh"),
            P("wsh", None),
            P("wsh", None),
            P("wsh"),
            P("wsh", None),
            P("wsh", None),
            P("wsh", "ctx", None),
        ),
        out_specs=(
            P("wsh", "ctx", None),
            P("wsh", "ctx", None),
            P("wsh"),
            P("wsh", None),
            P("wsh", None),
            P("wsh"),
            P("wsh", None),
            P("wsh", None),
        ),
        check_vma=False,
    )
```

profile of v0, /device:TPU:0, one launch (start us, length us, event | category | flops | bytes accessed | tf_op | source)
XLA Modules:
  0.0 708.5 jit_solution(2102755796486438782)
XLA Ops:
  10.2 4.8 collective-permute-start.2
  20.0 6.8 all-reduce.4
  33.0 10.2 %all-gather.5.cloned.1.call-done = bf16[768,2304]{1,0:T(8,128)(2,1)} async-done(((bf16[192,2304]{1,0:T(8,128)(2,1)}), bf16[768,2304]{1,0:T(8,128)(2,1)}) %all-gather.5.cloned.1.call-update) | async-done | bytes 3538960 | tf_op jit(solution)/shard_map/all_gather | solution.py:99
  43.2 5.8 copy.39
  49.0 6.1 fusion.40
  72.4 4.0 add_convert_fusion.3
  85.0 29.2 %collective-permute-done = bf16[4,64,1536]{2,1,0:T(8,128)(2,1)S(1)} collective-permute-done((bf16[4,64,1536]{2,1,0:T(8,128)(2,1)S(1)}, bf16[4,64,1536]{2,1,0:T(8,128)(2,1)S(1)}, u32[]{:S(2)}, u32[]{:S(2)}) %collective-permute-start) | collective-permute-done | bytes 786464 | tf_op jit(solution)/shard_map/ppermute | solution.py:23
  117.1 4.3 copy.46
  121.4 4.3 copy.45
  125.7 5.7 fusion.68
  131.4 4.9 fusion
  138.5 7.0 fusion.50
  152.9 10.7 %fusion.63 = f32[1024,2304]{1,0:T(8,128)} fusion(bf16[768,2304]{1,0:T(8,128)(2,1)} %all-gather.9.cloned.1.call-done, f32[1024,768]{1,0:T(8,128)} %copy-done.14, f32[768]{0:T(1024)S(1)} %convert_element_type.106, f32[1024]{0:T(1024)S(1)} %add_rsqrt_fusion, f32[1024]{0:T(1024)S(1)} %broadcast_multiply_fusion.8), kind=kOutput, calls=%fused_computation.151 | convolution fusion | flops 3627024384 | bytes 16133120 | tf_op jit(solution)/shard_map/dot_general | solution.py:156
  163.6 15.2 %add_convert_fusion = (bf16[1024,1152]{1,0:T(8,128)(2,1)S(1)}, f32[1024,1152]{1,0:T(8,128)S(1)}, f32[1024,1152]{1,0:T(8,128)S(1)}) fusion(f32[1024,2304]{1,0:T(8,128)} %fusion.63, bf16[1024,768]{1,0:T(8,128)(2,1)S(1)} %bitcast.139, bf16[1152,768]{1,0:T(8,128)(2,1)} %all-gather.11.cloned.1.call-done), kind=kOutput, calls=%fused_computation.24 | convolution fusion | flops 1898053632 | bytes 24576000 | tf_op jit(solution)/shard_map/dot_general | solution.py:82
  182.4 6.3 multiply_reduce_fusion.1
  195.1 14.2 %multiply_reduce_fusion = (f32[4,12,256]{2,1,0:T(8,128)S(1)}, f32[4,12,256,384]{3,2,1,0:T(8,128)}) fusion(f32[4,12,256,384]{3,2,1,0:T(8,128)} %copy-done, f32[4,12,256]{2,1,0:T(8,128)S(1)} %log_add_fusion, bf16[4,384,12,64]{1,3,2,0:T(8,128)(2,1)} %bitcast.122, bf16[4,256,12,64]{1,0,3,2:T(4,128)(2,1)S(1)} %reshape.263), kind=kOutput, calls=%fused_computation.1 | convolution fusion | flops 618123264 | bytes 41779200 | tf_op jit(solution)/shard_map/lqhd,lkhd->lhqk/dot_general | solution.py:182
  209.4 9.6 %fusion.2 = f32[4,12,64,384]{3,2,1,0:T(8,128)} fusion(f32[4,12,256,384]{3,2,1,0:T(8,128)} %copy-done, f32[4,12,256]{2,1,0:T(8,128)S(1)} %log_add_fusion, bf16[4,256,12,64]{1,0,3,2:T(4,128)(2,1)S(1)} %reshape.263), kind=kOutput, calls=%fused_computation.14 | convolution fusion | flops 613416960 | bytes 25214976 | tf_op jit(solution)/shard_map/lhqk,lqhd->lkhd/dot_general | solution.py:195
  222.8 9.6 %multiply_convert_fusion = bf16[4,12,256,384]{3,2,1,0:T(8,128)(2,1)S(1)} fusion(f32[4,12,256,384]{3,2,1,0:T(8,128)S(1)} %copy-done.1, f32[4,12,256,384]{3,2,1,0:T(8,128)} %copy-done, f32[4,12,256]{2,1,0:T(8,128)S(1)} %get-tuple-element.84, f32[4,12,256]{2,1,0:T(8,128)S(1)} %log_add_fusion), kind=kLoop, calls=%fused_computation | loop fusion | flops 18874368 | bytes 47284224 | tf_op jit(solution)/shard_map/convert_element_type | solution.py:186
  232.5 4.0 broadcast_multiply_fusion
  237.4 6.1 copy.52
  243.5 6.0 copy.53
  252.5 6.8 bitcast_multiply_fusion
  264.8 24.9 %collective-permute-done.4 = f32[4,64,1536]{2,1,0:T(8,128)S(1)} collective-permute-done((f32[4,64,1536]{2,1,0:T(8,128)S(1)}, f32[4,64,1536]{2,1,0:T(8,128)S(1)}, u32[]{:S(2)}, u32[]{:S(2)}) %collective-permute-start.4) | collective-permute-done | bytes 1572896 | tf_op jit(solution)/shard_map/ppermute | solution.py:32
  290.1 5.3 collective-permute-start.5
  302.1 7.1 fusion.34
  309.1 18.6 %collective-permute-done.5 = f32[4,64,1536]{2,1,0:T(8,128)S(1)} collective-permute-done((f32[4,64,1536]{2,1,0:T(8,128)S(1)}, f32[4,64,1536]{2,1,0:T(8,128)S(1)}, u32[]{:S(2)}, u32[]{:S(2)}) %collective-permute-start.5) | collective-permute-done | bytes 1572896 | tf_op jit(solution)/shard_map/ppermute | solution.py:32
  348.9 9.1 %fusion.32 = (f32[768]{0:T(1024)S(1)}, f32[1024]{0:T(1024)S(1)}, f32[1024]{0:T(1024)S(1)}, bf16[1024,768]{1,0:T(8,128)(2,1)S(1)}, f32[1024,768]{1,0:T(8,128)}) fusion(bf16[4,256,768]{2,1,0:T(8,128)(2,1)S(1)} %copy-done.12, f32[1024]{0:T(1024)S(1)} %bitcast.148, f32[1024]{0:T(1024)S(1)} %bitcast.146, f32[768]{0:T(1024)S(1)} %copy-done.40, ...), kind=kOutput, calls=%fused_computation.72 | convolution fusion | flops 3646682368 | bytes 14571520 | tf_op jit(solution)/shard_map/dot_general | solution.py:82
  358.0 9.2 %fusion.36 = f32[768,2304]{1,0:T(8,128)} fusion(bf16[1024,768]{1,0:T(8,128)(2,1)S(1)} %get-tuple-element.67, bf16[1024,768]{0,1:T(8,128)(2,1)S(1)} %copy-done.33, bf16[1024,768]{0,1:T(8,128)(2,1)S(1)} %copy-done.32, bf16[1024,768]{0,1:T(8,128)(2,1)S(1)} %bitcast.144), kind=kOutput, calls=%fused_computation.88 | convolution fusion | flops 3638034432 | bytes 13369344 | tf_op jit(solution)/shard_map/dot_general | solution.py:76
  367.3 6.5 add_convert_fusion.2
  373.8 43.8 %all-reduce.2 = (f32[768]{0:T(1024)S(1)}, f32[768]{0:T(1024)S(1)}) all-reduce(f32[768]{0:T(1024)S(1)} %get-tuple-element.34, f32[768]{0:T(1024)S(1)} %get-tuple-element.32), channel_id=1, replica_groups=mesh['ctx'=8,'wsh'=4] {'ctx','wsh'}, use_global_device_ids=true, to_apply=%region_12.13 | all-reduce | flops 1536 | bytes 12288 | tf_op jit(solution)/shard_map/psum | solution.py:229
  418.9 4.4 fusion.31
  423.3 268.6 %all-reduce.7.cloned.1.call-done = (f32[768,2304]{1,0:T(8,128)}, f32[768,768]{1,0:T(8,128)}, f32[768,2304]{1,0:T(8,128)}, f32[1152,768]{1,0:T(8,128)}) async-done(((f32[768,2304]{1,0:T(8,128)}, f32[768,768]{1,0:T(8,128)}, f32[768,2304]{1,0:T(8,128)}, f32[1152,768]{1,0:T(8,128)}), (f32[768,2304]{1,0:T(8,128)}, f32[768,768]{1,0:T(8,128)}, f32[768,2304]{1,0:T(8,128)}, ...) | async-done | bytes 20054032 | tf_op jit(solution)/shard_map/psum | solution.py:229
  (210 shorter events, 113.4 us)
Async XLA Ops:
  7.2 19.7 %copy-start.10 = (bf16[4,256,768]{2,1,0:T(8,128)(2,1)S(1)}, bf16[4,256,768]{2,1,0:T(8,128)(2,1)}, u32[]{:S(2)}) copy-start(bf16[4,256,768]{2,1,0:T(8,128)(2,1)} %param.13) | copy-start | bytes 4718596
  7.2 36.1 %all-gather.5.cloned.1.call-start = ((), (), s32[]{:S(2)}) async-start(), calls=%async_computation | async-start | bytes 4423680 | tf_op jit(solution)/shard_map/all_gather | solution.py:99
  7.9 139.3 %all-gather.7.cloned.1.call-start = ((), (), s32[]{:S(2)}) async-start(), calls=%async_computation.1 | async-start | bytes 1474560 | tf_op jit(solution)/shard_map/all_gather | solution.py:100
  8.7 144.2 %all-gather.9.cloned.1.call-start = ((), (), s32[]{:S(2)}) async-start(), calls=%async_computation.2 | async-start | bytes 4423680 | tf_op jit(solution)/shard_map/all_gather | solution.py:102
  9.4 154.1 %all-gather.11.cloned.1.call-start = ((), (), s32[]{:S(2)}) async-start(), calls=%async_computation.3 | async-start | bytes 2211840 | tf_op jit(solution)/shard_map/all_gather | solution.py:103
  10.2 71.6 %collective-permute-start.2 = (bf16[4,64]{1,0:T(4,128)(2,1)S(1)}, bf16[4,64]{1,0:T(4,128)(2,1)S(1)}, u32[]{:S(2)}, u32[]{:S(2)}) collective-permute-start(bf16[4,64]{1,0:T(4,128)(2,1)S(1)} %slice.128), channel_id=1, source_target_pairs={{0,4},{4,8},{8,12},{12,16},{16,20},{20,24},{24,28},{1,5},{5,9},{9,... | collective-permute-start | bytes 1544 | tf_op jit(solution)/shard_map/ppermute | solution.py:23
  15.0 66.7 %collective-permute-start.3 = (bf16[4,64]{1,0:T(4,128)(2,1)S(1)}, bf16[4,64]{1,0:T(4,128)(2,1)S(1)}, u32[]{:S(2)}, u32[]{:S(2)}) collective-permute-start(bf16[4,64]{1,0:T(4,128)(2,1)S(1)} %slice.128), channel_id=1, source_target_pairs={{4,0},{8,4},{12,8},{16,12},{20,16},{24,20},{28,24},{5,1},{9,5},{13... | collective-permute-start | bytes 1544 | tf_op jit(solution)/shard_map/ppermute | solution.py:24
  16.3 675.5 %all-reduce.7.cloned.1.call-start = ((), (), s32[]{:S(2)}) async-start(), calls=%async_computation.4 | async-start | bytes 40108032 | tf_op jit(solution)/shard_map/psum | solution.py:229
  26.9 22.2 %copy-start.39 = (f32[768]{0:T(1024)}, f32[768]{0:T(1024)S(1)}, u32[]{:S(2)}) copy-start(f32[768]{0:T(1024)S(1)} %convert_element_type.95) | copy-start | bytes 9220
  28.6 53.5 %copy-start.34 = (f32[256,64]{0,1:T(8,128)}, f32[256,64]{0,1:T(8,128)S(1)}, u32[]{:S(2)}) copy-start(f32[256,64]{0,1:T(8,128)S(1)} %get-tuple-element.71) | copy-start | bytes 196612
  76.6 37.7 %collective-permute-start = (bf16[4,64,1536]{2,1,0:T(8,128)(2,1)S(1)}, bf16[4,64,1536]{2,1,0:T(8,128)(2,1)S(1)}, u32[]{:S(2)}, u32[]{:S(2)}) collective-permute-start(bf16[4,64,1536]{2,1,0:T(8,128)(2,1)S(1)} %get-tuple-element.63), channel_id=1, source_target_pairs={{0,4},{4,8},{8,12},{12,16},{16,20},{20,24},{24,28},{1,5},{5,9},{9,... | collective-permute-start | bytes 2359304 | tf_op jit(solution)/shard_map/ppermute | solution.py:23
  80.3 34.0 %collective-permute-start.1 = (bf16[4,64,1536]{2,1,0:T(8,128)(2,1)S(1)}, bf16[4,64,1536]{2,1,0:T(8,128)(2,1)S(1)}, u32[]{:S(2)}, u32[]{:S(2)}) collective-permute-start(bf16[4,64,1536]{2,1,0:T(8,128)(2,1)S(1)} %get-tuple-element.64), channel_id=1, source_target_pairs={{4,0},{8,4},{12,8},{16,12},{20,16},{24,20},{28,24},{5,1},{9,5},{13... | collective-permute-start | bytes 2359304 | tf_op jit(solution)/shard_map/ppermute | solution.py:24
  82.2 32.1 %copy-start.9 = (bf16[4,256,768]{2,1,0:T(8,128)(2,1)S(1)}, bf16[4,256,768]{2,1,0:T(8,128)(2,1)}, u32[]{:S(2)}) copy-start(bf16[4,256,768]{2,1,0:T(8,128)(2,1)} %copy-done.8) | copy-start | bytes 4718596
  85.0 40.7 %copy-start.5 = (bf16[4,256,12,64]{1,3,2,0:T(8,128)(2,1)}, bf16[4,256,12,64]{1,3,2,0:T(8,128)(2,1)S(1)}, u32[]{:S(2)}) copy-start(bf16[4,256,12,64]{1,3,2,0:T(8,128)(2,1)S(1)} %fusion.15) | copy-start | bytes 4718596
  131.4 7.1 %copy-start = (f32[4,12,256,384]{3,2,1,0:T(8,128)}, f32[4,12,256,384]{3,2,1,0:T(8,128)S(1)}, u32[]{:S(2)}) copy-start(f32[4,12,256,384]{3,2,1,0:T(8,128)S(1)} %get-tuple-element.79) | copy-start | bytes 56623108
  131.4 7.1 copy-start.7
  152.8 10.7 %copy-start.27 = (bf16[4,256,768]{2,1,0:T(8,128)(2,1)S(1)}, bf16[4,256,768]{2,1,0:T(8,128)(2,1)}, u32[]{:S(2)}) copy-start(bf16[4,256,768]{2,1,0:T(8,128)(2,1)} %param.21) | copy-start | bytes 4718596
  163.5 15.3 %slice-start.4 = ((s8[9437184]{0:T(1024)(128)(4,1)}), s8[4194304]{0:T(1024)(128)(4,1)S(1)}, s32[]{:S(2)}) async-start(s8[9437184]{0:T(1024)(128)(4,1)} %bitcast.128), calls=%async_computation.9 | async-start | bytes 8388608
  163.5 15.3 %slice-start.5 = ((s8[9437184]{0:T(1024)(128)(4,1)}), s8[4194304]{0:T(1024)(128)(4,1)S(1)}, s32[]{:S(2)}) async-start(s8[9437184]{0:T(1024)(128)(4,1)} %bitcast.128), calls=%async_computation.10 | async-start | bytes 8388608
  163.5 15.3 %slice-start.6 = ((s8[9437184]{0:T(1024)(128)(4,1)}), s8[1048576]{0:T(1024)(128)(4,1)S(1)}, s32[]{:S(2)}) async-start(s8[9437184]{0:T(1024)(128)(4,1)} %bitcast.128), calls=%async_computation.11 | async-start | bytes 2097152
  181.6 7.1 copy-start.25
  209.4 13.4 %copy-start.1 = (f32[4,12,256,384]{3,2,1,0:T(8,128)S(1)}, f32[4,12,256,384]{3,2,1,0:T(8,128)}, u32[]{:S(2)}) copy-start(f32[4,12,256,384]{3,2,1,0:T(8,128)} %get-tuple-element.85) | copy-start | bytes 56623108
  222.8 9.6 %copy-start.6 = (bf16[4,256,12,64]{1,3,2,0:T(8,128)(2,1)S(1)}, bf16[4,256,12,64]{1,3,2,0:T(8,128)(2,1)}, u32[]{:S(2)}) copy-start(bf16[4,256,12,64]{1,3,2,0:T(8,128)(2,1)} %copy-done.5) | copy-start | bytes 4718596
  251.2 38.5 %collective-permute-start.4 = (f32[4,64,1536]{2,1,0:T(8,128)S(1)}, f32[4,64,1536]{2,1,0:T(8,128)S(1)}, u32[]{:S(2)}, u32[]{:S(2)}) collective-permute-start(f32[4,64,1536]{2,1,0:T(8,128)S(1)} %fusion.42), channel_id=1, source_target_pairs={{4,0},{8,4},{12,8},{16,12},{20,16},{24,20},{28,24},{5,1},{9,5},{13... | collective-permute-start | bytes 4718600 | tf_op jit(solution)/shard_map/ppermute | solution.py:32
  264.7 30.7 %copy-start.18 = (f32[1024,768]{1,0:T(8,128)S(1)}, f32[1024,768]{1,0:T(8,128)}, u32[]{:S(2)}) copy-start(f32[1024,768]{1,0:T(8,128)} %copy-done.17) | copy-start | bytes 9437188
  264.8 30.7 %copy-start.30 = (bf16[96,8,4,256]{3,1,2,0:T(8,128)(2,1)S(1)}, bf16[96,8,4,256]{3,1,2,0:T(8,128)(2,1)}, u32[]{:S(2)}) copy-start(bf16[96,8,4,256]{3,1,2,0:T(8,128)(2,1)} %copy-done.29) | copy-start | bytes 4718596
  290.0 8.2 %copy-start.24 = (bf16[1024,1152]{1,0:T(8,128)(2,1)S(1)}, bf16[1024,1152]{1,0:T(8,128)(2,1)}, u32[]{:S(2)}) copy-start(bf16[1024,1152]{1,0:T(8,128)(2,1)} %get-tuple-element.49) | copy-start | bytes 7077892
  290.0 8.2 %copy-start.28 = (bf16[4,256,768]{2,1,0:T(8,128)(2,1)S(1)}, bf16[4,256,768]{2,1,0:T(8,128)(2,1)}, u32[]{:S(2)}) copy-start(bf16[4,256,768]{2,1,0:T(8,128)(2,1)} %param.21) | copy-start | bytes 4718596
  290.1 37.7 %collective-permute-start.5 = (f32[4,64,1536]{2,1,0:T(8,128)S(1)}, f32[4,64,1536]{2,1,0:T(8,128)S(1)}, u32[]{:S(2)}, u32[]{:S(2)}) collective-permute-start(f32[4,64,1536]{2,1,0:T(8,128)S(1)} %get-tuple-element.50), channel_id=1, source_target_pairs={{0,4},{4,8},{8,12},{12,16},{16,20},{20,24},{24,28},{1,5},{5,9},{9,... | collective-permute-start | bytes 4718600 | tf_op jit(solution)/shard_map/ppermute | solution.py:32
  348.8 9.2 %copy-start.31 = (bf16[96,8,4,256]{3,1,2,0:T(8,128)(2,1)S(1)}, bf16[96,8,4,256]{3,1,2,0:T(8,128)(2,1)}, u32[]{:S(2)}) copy-start(bf16[96,8,4,256]{3,1,2,0:T(8,128)(2,1)} %copy.61) | copy-start | bytes 4718596
  348.9 9.2 %copy-start.32 = (bf16[1024,768]{0,1:T(8,128)(2,1)S(1)}, bf16[1024,768]{0,1:T(8,128)(2,1)}, u32[]{:S(2)}) copy-start(bf16[1024,768]{0,1:T(8,128)(2,1)} %copy.56) | copy-start | bytes 4718596
  348.9 9.2 %copy-start.33 = (bf16[1024,768]{0,1:T(8,128)(2,1)S(1)}, bf16[1024,768]{0,1:T(8,128)(2,1)}, u32[]{:S(2)}) copy-start(bf16[1024,768]{0,1:T(8,128)(2,1)} %copy.57) | copy-start | bytes 4718596
  (32 other events, 112.7 us)
Sparse Core Ops, SparseCore 0:
  9.6 33.6 all-gather.4
  44.8 17.4 all-gather.6
  63.8 30.7 all-gather.8
  96.0 20.7 all-gather.10
  367.4 324.4 all-reduce.6
where the time goes:
time: 717 us; the launch traced here: 708 us
  waiting for transfers between devices  354 us (49%)
  matrix products  129 us (18%)
  local copies, waits for them, and re-layouts  92.8 us (13%)
  blocking collectives  50.6 us (7%)
  other arithmetic  48.3 us (7%)
  starting transfers between devices  18.1 us (3%)
  between operations  15.8 us (2%)
    psum x1, waiting for transfers between devices, per_device(): lax.psum((partials[0], partials[1], partials[2], partials[3], partials[4]...  269 us
    psum x1, blocking collectives, per_device(): lax.psum((partials[0], partials[1], partials[2], partials[3], partials[4]...  43.8 us
    ppermute x2, waiting for transfers between devices, passed_along(): return lax.ppermute(value, axis, pairs)  43.5 us
    dot_general x4, matrix products, against(): lax.dot_general(left, right, (((1,), (1,)), ((), ())), preferred_element_...  32.1 us
    ppermute x2, waiting for transfers between devices, extended(): before = lax.ppermute(last, axis, up)  29.2 us
    dot_general x4, matrix products, contract_rows(): lax.dot_general(left, right, (((0,), (0,)), ((), ())), preferred_element_...  22.9 us
    unnamed x115, local copies, waits for them, and re-layouts  20.3 us
  transfers between devices with their start and end apart: 11, of which 5 were waited for; matrix products, arithmetic and copies ran while one was open for 18% of the time, Pallas kernels for 0%

commit v1 on v0

v1 whole, which is shorter than its diff:
```python
import functools
import math

import jax
import jax.numpy as jnp
from jax import lax
from jax.experimental import pallas as pl
from jax.experimental.pallas import tpu as pltpu
from jax.sharding import PartitionSpec as P

HEAD = 64
HALF = 64
EPS = 1e-05
THETA = 10000.0
MASKED = -1e30
PAIR = 2 * HEAD
QROWS = 128
WIN = QROWS + 2 * HALF
VMEM_BYTES = 56 * 1024 * 1024

F32 = jnp.float32
BF16 = jnp.bfloat16


def dot_nn(left, right):
    return jnp.dot(left, right, preferred_element_type=F32)


def dot_nt(left, right):
    return lax.dot_general(left, right, (((1,), (1,)), ((), ())), preferred_element_type=F32)


def dot_tn(left, right):
    return lax.dot_general(left, right, (((0,), (0,)), ((), ())), preferred_element_type=F32)


def swap(value, axis, bit):
    peers = lax.axis_size(axis)
    return lax.ppermute(value, axis, [(i, i ^ bit) for i in range(peers)])


def shifted(value, axis, by):
    peers = lax.axis_size(axis)
    return lax.ppermute(value, axis, [(i, i + by) for i in range(peers) if 0 <= i + by < peers])


def tied(value, *after):
    return lax.optimization_barrier((value,) + after)[0]


def shards_of(shard):
    near = swap(shard, "wsh", 1)
    far = swap(shard, "wsh", 2)
    far_near = swap(far, "wsh", 1)
    return (shard, near, far, far_near)


def pick(value, index, axis=0):
    return lax.dynamic_index_in_dim(value, index, axis, keepdims=False)


def added(kept, *received):
    total = kept.astype(F32)
    for item in received:
        total = total + item.astype(F32)
    return total.astype(BF16)


def reduced(grad):
    me_w, me_c = lax.axis_index("wsh"), lax.axis_index("ctx")
    rows, cols = grad.shape[0] // 4, grad.shape[1]
    core, side = me_w % 2, me_w // 2
    quarters = grad.reshape(2, 2, rows, cols)
    got = swap(pick(quarters, 1 - core, 1), "wsh", 1)
    pair = added(pick(quarters, core, 1), got)
    got = swap(pick(pair, 1 - side), "wsh", 2)
    mine = added(pick(pair, side), got)
    if lax.axis_size("ctx") != 8:
        return lax.psum(mine.astype(F32), "ctx")
    at_x, at_z = me_c % 2, me_c // 2
    half = cols // 2
    halves = lambda index: lax.dynamic_slice_in_dim(mine, index * half, half, 1)
    got = swap(halves(1 - at_x), "ctx", 1)
    part = added(halves(at_x), got)
    chunk = rows // 4
    chunks = lambda index: lax.dynamic_slice_in_dim(part, index * chunk, chunk, 0)
    got = [swap(chunks(at_z ^ d), "ctx", 2 * d) for d in (1, 2, 3)]
    own = added(chunks(at_z), *got)
    whole = jnp.zeros((rows, half), BF16)
    whole = lax.dynamic_update_slice_in_dim(whole, own, at_z * chunk, 0)
    for d in (1, 2, 3):
        whole = lax.dynamic_update_slice_in_dim(whole, swap(own, "ctx", 2 * d), (at_z ^ d) * chunk, 0)
    other = swap(whole, "ctx", 1)
    low = jnp.where(at_x == 0, whole, other)
    high = jnp.where(at_x == 0, other, whole)
    return jnp.concatenate([low, high], axis=1).astype(F32)


def reduced_small(value):
    if lax.axis_size("ctx") != 8:
        return lax.psum(value, ("ctx", "wsh"))
    for axis, bit in (("wsh", 1), ("wsh", 2), ("ctx", 1), ("ctx", 2), ("ctx", 4)):
        value = value + swap(value, axis, bit)
    return value


def stage_weight(me, shards, scratch, sems):
    rows = shards[0].shape[0]
    return [
        pltpu.make_async_copy(
            shard, scratch.at[pl.ds(pl.multiple_of((me ^ k) * rows, rows), rows)], sems.at[k]
        )
        for k, shard in enumerate(shards)
    ]


def norm_of(values):
    average = jnp.mean(values, axis=-1, keepdims=True)
    centred = values - average
    inverse = lax.rsqrt(jnp.mean(centred * centred, axis=-1, keepdims=True) + EPS)
    return centred * inverse, inverse


def norm_back(incoming, normal, inverse, gain):
    scaled = incoming * gain
    return inverse * (
        scaled
        - jnp.mean(scaled, axis=-1, keepdims=True)
        - normal * jnp.mean(scaled * normal, axis=-1, keepdims=True)
    )


def head_lanes():
    lane = lax.broadcasted_iota(jnp.int32, (1, PAIR), 1)
    return lane, lane < HEAD


def turned(value, lane):
    ahead = pltpu.roll(value, PAIR - HEAD // 2, 1)
    behind = pltpu.roll(value, HEAD // 2, 1)
    return jnp.where(lane % HEAD < HEAD // 2, ahead, behind)


def stacked(value, first, scale):
    one = jnp.where(first, scale, 0.0).astype(BF16)
    two = jnp.where(first, 0.0, scale).astype(BF16)
    return jnp.concatenate([value * one, value * two], axis=0)


def attend_kernel(
    me_ref, left_ok, right_ok, x_ref, hl_ref, hr_ref, gain_ref, cos_ref, sin_ref, s0, s1, s2, s3,
    q_ref, kv_ref, first_ref, probs_ref, mixed_ref, w_ref, sems,
):
    pack = pl.program_id(0)
    block = x_ref.shape[1]
    width = x_ref.shape[2]
    span = block + 2 * HALF

    @pl.when(pack == 0)
    def _():
        copies = stage_weight(me_ref[0], (s0, s1, s2, s3), w_ref, sems)
        for copy in copies:
            copy.start()
        for copy in copies:
            copy.wait()

    values = jnp.concatenate([hl_ref[0], x_ref[0], hr_ref[0]], axis=0).astype(F32)
    normal, _ = norm_of(values)
    first_ref[0] = (normal * gain_ref[...]).astype(BF16)
    lane, first = head_lanes()
    cos, sin = cos_ref[...], sin_ref[...]
    own = slice(HALF, HALF + block)
    step = 2 * PAIR
    for j in range(width // step):
        cols = slice(j * step, (j + 1) * step)
        q = dot_nn(first_ref[0, own, :], w_ref[:, cols])
        k = dot_nn(first_ref[0], w_ref[:, width + j * step : width + (j + 1) * step])
        v = dot_nn(first_ref[0], w_ref[:, 2 * width + j * step : 2 * width + (j + 1) * step])
        for i in range(2):
            part = slice(i * PAIR, (i + 1) * PAIR)
            base = j * step + i * PAIR
            qp, kp = q[:, part], k[:, part]
            q_ref[0, :, base : base + PAIR] = (
                qp * cos[own] + turned(qp, lane) * sin[own]
            ).astype(BF16)
            kv_ref[0, :, base : base + PAIR] = (kp * cos + turned(kp, lane) * sin).astype(BF16)
        kv_ref[0, :, width + j * step : width + (j + 1) * step] = v.astype(BF16)

    row = lax.broadcasted_iota(jnp.int32, (QROWS, WIN), 0)
    col = lax.broadcasted_iota(jnp.int32, (QROWS, WIN), 1)
    near = (col >= row) & (col <= row + 2 * HALF)
    blocks = block // QROWS
    for b in range(blocks):
        allowed = near
        if b == 0:
            allowed = allowed & ((col >= HALF) | (left_ok[pack] > 0))
        if b == blocks - 1:
            allowed = allowed & ((col < WIN - HALF) | (right_ok[pack] > 0))
        bias = jnp.where(allowed, 0.0, MASKED)
        bias = jnp.concatenate([bias, bias], axis=0)
        rows = slice(b * QROWS, (b + 1) * QROWS)
        window = slice(b * QROWS, b * QROWS + WIN)
        for p in range(width // PAIR):
            cols = slice(p * PAIR, (p + 1) * PAIR)
            q2 = stacked(q_ref[0, rows, cols], first, HEAD ** -0.5)
            scores = dot_nt(q2, kv_ref[0, window, cols]) + bias
            powers = jnp.exp(scores - jnp.max(scores, axis=-1, keepdims=True))
            probs = (powers * (1.0 / jnp.sum(powers, axis=-1, keepdims=True))).astype(BF16)
            probs_ref[0, p, b] = probs
            out = dot_nn(probs, kv_ref[0, window, width + p * PAIR : width + (p + 1) * PAIR])
            mixed_ref[0, rows, cols] = jnp.where(first, out[:QROWS], out[QROWS:]).astype(BF16)


def attention_forward(me, left_ok, right_ok, tokens, halo_left, halo_right, gain, cos, sin, shards):
    packs, block, width = tokens.shape
    span = block + 2 * HALF
    pairs, blocks = width // PAIR, block // QROWS
    per_pack = lambda *dims: pl.BlockSpec((1,) + dims, lambda i: (i,) + (0,) * len(dims))
    fixed = lambda *dims: pl.BlockSpec(dims, lambda i: (0,) * len(dims))
    smem = pl.BlockSpec(memory_space=pltpu.SMEM)
    return pl.pallas_call(
        attend_kernel,
        grid=(packs,),
        in_specs=[smem] * 3
        + [per_pack(block, width), per_pack(HALF, width), per_pack(HALF, width)]
        + [fixed(1, width), fixed(span, PAIR), fixed(span, PAIR)]
        + [pl.BlockSpec(memory_space=pl.ANY)] * 4,
        out_specs=[
            per_pack(block, width),
            per_pack(span, 2 * width),
            per_pack(span, width),
            per_pack(pairs, blocks, 2 * QROWS, WIN),
            per_pack(block, width),
        ],
        out_shape=[
            jax.ShapeDtypeStruct((packs, block, width), BF16),
            jax.ShapeDtypeStruct((packs, span, 2 * width), BF16),
            jax.ShapeDtypeStruct((packs, span, width), BF16),
            jax.ShapeDtypeStruct((packs, pairs, blocks, 2 * QROWS, WIN), BF16),
            jax.ShapeDtypeStruct((packs, block, width), BF16),
        ],
        scratch_shapes=[
            pltpu.VMEM((width, 3 * width), BF16),
            pltpu.SemaphoreType.DMA((4,)),
        ],
        compiler_params=pltpu.CompilerParams(vmem_limit_bytes=VMEM_BYTES),
        cost_estimate=pl.CostEstimate(flops=7_000_000_000, bytes_accessed=30_000_000, transcendentals=0),
        name="attend",
    )(me, left_ok, right_ok, tokens, halo_left, halo_right, gain, cos, sin, *shards)


def mlp_kernel(
    me_ref, x_ref, mixed_ref, up_ref, gain_ref, o0, o1, o2, o3, i0, i1, i2, i3, d0, d1, d2, d3,
    out_ref, second_ref, hidden_ref, ggu_ref, gm_ref, low_ref, gmix_ref, ggain_ref,
    wo_ref, wi_ref, wd_ref, sems,
):
    tile = pl.program_id(0)
    ff = wd_ref.shape[0]
    copies = [
        stage_weight(me_ref[0], group, scratch, sems.at[n])
        for n, (group, scratch) in enumerate(
            (((o0, o1, o2, o3), wo_ref), ((i0, i1, i2, i3), wi_ref), ((d0, d1, d2, d3), wd_ref))
        )
    ]

    @pl.when(tile == 0)
    def _():
        for group in copies:
            for copy in group:
                copy.start()
        ggain_ref[...] = jnp.zeros_like(ggain_ref)
        for group in copies:
            for copy in group:
                copy.wait()

    gain = gain_ref[...]
    middle = x_ref[0].astype(F32) + dot_nn(mixed_ref[0], wo_ref[...])
    normal, inverse = norm_of(middle)
    second = (normal * gain).astype(BF16)
    second_ref[0] = second
    upstream = up_ref[0]
    step = 384
    result = middle
    for j in range(ff // step):
        cols = slice(j * step, (j + 1) * step)
        ups = slice(ff + j * step, ff + (j + 1) * step)
        gate = dot_nn(second, wi_ref[:, cols])
        up = dot_nn(second, wi_ref[:, ups])
        grad_hidden = dot_nt(upstream, wd_ref[cols, :])
        cumulative = 0.5 + 0.5 * lax.erf(gate * (0.5 ** 0.5))
        activated = gate * cumulative
        density = jnp.exp(-0.5 * gate * gate) * (1.0 / math.sqrt(2.0 * math.pi))
        hidden = (activated * up).astype(BF16)
        hidden_ref[0, :, cols] = hidden
        ggu_ref[0, :, cols] = (grad_hidden * up * (cumulative + gate * density)).astype(BF16)
        ggu_ref[0, :, ups] = (grad_hidden * activated).astype(BF16)
        result = result + dot_nn(hidden, wd_ref[cols, :])
    out_ref[0] = result.astype(BF16)
    grad_second = dot_nt(ggu_ref[0], wi_ref[...])
    ggain_ref[...] += jnp.sum(grad_second * normal, axis=0, keepdims=True)
    grad_middle = upstream.astype(F32) + norm_back(grad_second, normal, inverse, gain)
    gm_ref[0] = grad_middle
    low = grad_middle.astype(BF16)
    low_ref[0] = low
    gmix_ref[0] = dot_nt(low, wo_ref[...]).astype(BF16)


def feed_forward(me, tokens, mixed, upstream, gain, out_shards, in_shards, down_shards):
    packs, block, width = tokens.shape
    ff = 4 * down_shards[0].shape[0]
    per_pack = lambda *dims: pl.BlockSpec((1,) + dims, lambda i: (i,) + (0,) * len(dims))
    fixed = lambda *dims: pl.BlockSpec(dims, lambda i: (0,) * len(dims))
    smem = pl.BlockSpec(memory_space=pltpu.SMEM)
    shape = lambda dtype, *dims: jax.ShapeDtypeStruct((packs, block) + dims, dtype)
    return pl.pallas_call(
        mlp_kernel,
        grid=(packs,),
        in_specs=[smem]
        + [per_pack(block, width)] * 3
        + [fixed(1, width)]
        + [pl.BlockSpec(memory_space=pl.ANY)] * 12,
        out_specs=[
            per_pack(block, width),
            per_pack(block, width),
            per_pack(block, ff),
            per_pack(block, 2 * ff),
            per_pack(block, width),
            per_pack(block, width),
            per_pack(block, width),
            fixed(1, width),
        ],
        out_shape=[
            shape(BF16, width),
            shape(BF16, width),
            shape(BF16, ff),
            shape(BF16, 2 * ff),
            shape(F32, width),
            shape(BF16, width),
            shape(BF16, width),
            jax.ShapeDtypeStruct((1, width), F32),
        ],
        scratch_shapes=[
            pltpu.VMEM((width, width), BF16),
            pltpu.VMEM((width, 2 * ff), BF16),
            pltpu.VMEM((ff, width), BF16),
            pltpu.SemaphoreType.DMA((3, 4)),
        ],
        compiler_params=pltpu.CompilerParams(vmem_limit_bytes=VMEM_BYTES),
        cost_estimate=pl.CostEstimate(flops=14_000_000_000, bytes_accessed=40_000_000, transcendentals=0),
        name="feed_forward",
    )(me, tokens, mixed, upstream, gain, *out_shards, *in_shards, *down_shards)


def attend_back_kernel(
    me_ref, q_ref, kv_ref, probs_ref, gmix_ref, x_ref, hl_ref, hr_ref, cos_ref, sin_ref,
    s0, s1, s2, s3,
    dq_ref, dkv_ref, own_ref, left_ref, right_ref, ggain_ref, w_ref, sems,
):
    pack = pl.program_id(0)
    block, width = q_ref.shape[1], q_ref.shape[2]
    span = block + 2 * HALF
    copies = stage_weight(me_ref[0], (s0, s1, s2, s3), w_ref, sems)

    @pl.when(pack == 0)
    def _():
        for copy in copies:
            copy.start()
        ggain_ref[...] = jnp.zeros_like(ggain_ref)
        for copy in copies:
            copy.wait()

    lane, first = head_lanes()
    cos, sin = cos_ref[...], -sin_ref[...]
    own = slice(HALF, HALF + block)
    blocks = block // QROWS
    for p in range(width // PAIR):
        cols = slice(p * PAIR, (p + 1) * PAIR)
        vcols = slice(width + p * PAIR, width + (p + 1) * PAIR)
        dqs, dks, dvs = [], [], []
        for b in range(blocks):
            rows = slice(b * QROWS, (b + 1) * QROWS)
            window = slice(b * QROWS, b * QROWS + WIN)
            q2 = stacked(q_ref[0, rows, cols], first, HEAD ** -0.5)
            do2 = stacked(gmix_ref[0, rows, cols], first, 1.0)
            probs = probs_ref[0, p, b]
            wide = probs.astype(F32)
            dprobs = dot_nt(do2, kv_ref[0, window, vcols])
            inner = jnp.sum(dprobs * wide, axis=-1, keepdims=True)
            ds = (wide * (dprobs - inner)).astype(BF16)
            dq2 = dot_nn(ds, kv_ref[0, window, cols])
            dqs.append(jnp.where(first, dq2[:QROWS], dq2[QROWS:]) * (HEAD ** -0.5))
            dks.append(dot_tn(ds, q2))
            dvs.append(dot_tn(probs, do2))
        dq = jnp.concatenate(dqs, axis=0)
        over = WIN - QROWS
        merge = lambda a, b: jnp.concatenate([a[:QROWS], a[QROWS:] + b[:over], b[over:]], axis=0)
        dk, dv = merge(*dks), merge(*dvs)
        dq_ref[0, :, cols] = (dq * cos[own] + turned(dq, lane) * sin[own]).astype(BF16)
        dkv_ref[0, :, cols] = (dk * cos + turned(dk, lane) * sin).astype(BF16)
        dkv_ref[0, :, vcols] = dv.astype(BF16)
    halo = dot_nt(dkv_ref[0], w_ref[:, width:])
    own_grad = halo[own] + dot_nt(dq_ref[0], w_ref[:, :width])
    own_ref[0] = own_grad
    left_ref[0] = halo[:HALF].astype(BF16)
    right_ref[0] = halo[HALF + block :].astype(BF16)
    values = jnp.concatenate([hl_ref[0], x_ref[0], hr_ref[0]], axis=0).astype(F32)
    normal, _ = norm_of(values)
    ggain_ref[...] += (
        jnp.sum(own_grad * normal[own], axis=0, keepdims=True)
        + jnp.sum(halo[:HALF] * normal[:HALF], axis=0, keepdims=True)
        + jnp.sum(halo[HALF + block :] * normal[HALF + block :], axis=0, keepdims=True)
    )


def attention_back(me, q, kv, probs, gmix, tokens, halo_left, halo_right, cos, sin, shards):
    packs, block, width = q.shape
    span = block + 2 * HALF
    pairs, blocks = width // PAIR, block // QROWS
    per_pack = lambda *dims: pl.BlockSpec((1,) + dims, lambda i: (i,) + (0,) * len(dims))
    fixed = lambda *dims: pl.BlockSpec(dims, lambda i: (0,) * len(dims))
    smem = pl.BlockSpec(memory_space=pltpu.SMEM)
    return pl.pallas_call(
        attend_back_kernel,
        grid=(packs,),
        in_specs=[
            smem,
            per_pack(block, width),
            per_pack(span, 2 * width),
            per_pack(pairs, blocks, 2 * QROWS, WIN),
            per_pack(block, width),
            per_pack(block, width),
            per_pack(HALF, width),
            per_pack(HALF, width),
            fixed(span, PAIR),
            fixed(span, PAIR),
        ]
        + [pl.BlockSpec(memory_space=pl.ANY)] * 4,
        out_specs=[
            per_pack(block, width),
            per_pack(span, 2 * width),
            per_pack(block, width),
            per_pack(HALF, width),
            per_pack(HALF, width),
            fixed(1, width),
        ],
        out_shape=[
            jax.ShapeDtypeStruct((packs, block, width), BF16),
            jax.ShapeDtypeStruct((packs, span, 2 * width), BF16),
            jax.ShapeDtypeStruct((packs, block, width), F32),
            jax.ShapeDtypeStruct((packs, HALF, width), BF16),
            jax.ShapeDtypeStruct((packs, HALF, width), BF16),
            jax.ShapeDtypeStruct((1, width), F32),
        ],
        scratch_shapes=[
            pltpu.VMEM((width, 3 * width), BF16),
            pltpu.SemaphoreType.DMA((4,)),
        ],
        compiler_params=pltpu.CompilerParams(vmem_limit_bytes=VMEM_BYTES),
        cost_estimate=pl.CostEstimate(flops=9_000_000_000, bytes_accessed=30_000_000, transcendentals=0),
        name="attend_back",
    )(me, q, kv, probs, gmix, tokens, halo_left, halo_right, cos, sin, *shards)


def finish_kernel(x_ref, own_ref, fl_ref, fr_ref, gm_ref, gain_ref, out_ref):
    block = x_ref.shape[1]
    normal, inverse = norm_of(x_ref[0].astype(F32))
    grad = own_ref[0]
    grad = jnp.concatenate(
        [
            grad[:HALF] + fl_ref[0].astype(F32),
            grad[HALF : block - HALF],
            grad[block - HALF :] + fr_ref[0].astype(F32),
        ],
        axis=0,
    )
    out_ref[0] = (gm_ref[0] + norm_back(grad, normal, inverse, gain_ref[...])).astype(BF16)


def finish(tokens, own, from_left, from_right, grad_middle, gain):
    packs, block, width = tokens.shape
    per_pack = lambda *dims: pl.BlockSpec((1,) + dims, lambda i: (i,) + (0,) * len(dims))
    return pl.pallas_call(
        finish_kernel,
        grid=(packs,),
        in_specs=[
            per_pack(block, width),
            per_pack(block, width),
            per_pack(HALF, width),
            per_pack(HALF, width),
            per_pack(block, width),
            pl.BlockSpec((1, width), lambda i: (0, 0)),
        ],
        out_specs=per_pack(block, width),
        out_shape=jax.ShapeDtypeStruct((packs, block, width), BF16),
        cost_estimate=pl.CostEstimate(flops=20_000_000, bytes_accessed=10_000_000, transcendentals=0),
        name="finish",
    )(tokens, own, from_left, from_right, grad_middle, gain)


def tables(start, count):
    half_size = HEAD // 2
    freqs = jnp.power(THETA, -jnp.arange(half_size, dtype=F32) * (2.0 / HEAD))
    positions = (start + jnp.arange(count, dtype=jnp.int32)).astype(F32)
    angles = positions[:, None] * freqs[None, :]
    cos, sin = jnp.cos(angles), jnp.sin(angles)
    return (
        jnp.concatenate([cos, cos, cos, cos], axis=-1),
        jnp.concatenate([-sin, sin, -sin, sin], axis=-1),
    )


def weight_grad(left, right):
    return dot_tn(
        left.reshape(-1, left.shape[-1]), right.reshape(-1, right.shape[-1])
    ).astype(BF16)


def per_device(tokens, doc_begin, gain_attn, w_qkv, w_att_out, gain_mlp, w_in, w_down, cotangent):
    packs, block, width = tokens.shape
    me_w, me_c = lax.axis_index("wsh"), lax.axis_index("ctx")
    me = me_w.reshape(1).astype(jnp.int32)

    gains = jnp.stack([gain_attn, gain_mlp])
    gain_parts = shards_of(gains)
    qkv_shards = shards_of(w_qkv)
    halo_left = shifted(tokens[:, block - HALF :], "ctx", 1)
    halo_right = shifted(tokens[:, :HALF], "ctx", -1)
    doc_right = shifted(doc_begin, "ctx", -1)
    gain_full = jnp.zeros((2, 4, gains.shape[1]), F32)
    for k, part in enumerate(gain_parts):
        gain_full = lax.dynamic_update_slice_in_dim(
            gain_full, part.astype(F32)[:, None], me_w ^ k, 1
        )
    gain_full = gain_full.reshape(2, width)
    gain_one, gain_two = gain_full[:1], gain_full[1:]
    left_ok = (doc_begin[:, 0] < me_c).astype(jnp.int32)
    right_ok = (
        (doc_right[:, 0] == doc_begin[:, 0]) & (me_c + 1 < lax.axis_size("ctx"))
    ).astype(jnp.int32)
    cos, sin = tables(me_c * block - HALF, block + 2 * HALF)

    out_shards = shards_of(tied(w_att_out, qkv_shards[2]))
    in_shards = shards_of(tied(w_in, out_shards[2]))
    down_shards = shards_of(tied(w_down, in_shards[2]))

    q, kv, first_in, probs, mixed = attention_forward(
        me, left_ok, right_ok, tokens, halo_left, halo_right, gain_one, cos, sin, qkv_shards
    )
    output, second_in, hidden, ggu, grad_middle, low, gmix, ggain_two = feed_forward(
        me, tokens, mixed, cotangent, gain_two, out_shards, in_shards, down_shards
    )
    grad_in = reduced(weight_grad(second_in, ggu))
    grad_down = reduced(weight_grad(hidden, cotangent))
    grad_out = reduced(weight_grad(mixed, low))
    dq, dkv, own, to_left, to_right, ggain_one = attention_back(
        me, q, kv, probs, gmix, tokens, halo_left, halo_right, cos, sin, qkv_shards
    )
    from_right = shifted(to_left, "ctx", -1)
    from_left = shifted(to_right, "ctx", 1)
    grad_qkv = reduced(
        jnp.concatenate(
            [weight_grad(first_in[:, HALF : HALF + block], dq), weight_grad(first_in, dkv)], axis=1
        )
    )
    grad_gains = reduced_small(jnp.concatenate([ggain_one, ggain_two], axis=0))
    grad_gains = lax.dynamic_slice_in_dim(grad_gains, me_w * gains.shape[1], gains.shape[1], 1)
    grad_tokens = finish(tokens, own, from_left, from_right, grad_middle, gain_one)
    return (
        output, grad_tokens, grad_gains[0], grad_qkv, grad_out, grad_gains[1], grad_in, grad_down,
    )


def solution(mesh):
    return jax.shard_map(
        per_device,
        mesh=mesh,
        in_specs=(
            P("wsh", "ctx", None),
            P("wsh", "ctx"),
            P("wsh"),
            P("wsh", None),
            P("wsh", None),
            P("wsh"),
            P("wsh", None),
            P("wsh", None),
            P("wsh", "ctx", None),
        ),
        out_specs=(
            P("wsh", "ctx", None),
            P("wsh", "ctx", None),
            P("wsh"),
            P("wsh", None),
            P("wsh", None),
            P("wsh"),
            P("wsh", None),
            P("wsh", None),
        ),
        check_vma=False,
    )
```

time: 717 us -> 346 us (0.48); the launches traced: 708 us -> 345 us
  waiting for transfers between devices: 354 us -> 108 us
  matrix products: 129 us -> 18.5 us
  Pallas kernels: 0 us -> 85.1 us
  starting transfers between devices: 18.1 us -> 92.6 us
  local copies, waits for them, and re-layouts: 92.8 us -> 19.2 us
  blocking collectives: 50.6 us -> 0 us
  other arithmetic: 48.3 us -> 20.3 us
  between operations: 15.8 us -> 1.49 us
    psum x1 -> x0, waiting for transfers between devices: 269 us -> none  [per_device(): lax.psum((partials[0], partials[1], partials[2], partials[3], partials[4]...]
    dot_general x18 -> x5, matrix products: 129 us -> 18.5 us  [dot_tn(): lax.dot_general(left, right, (((0,), (0,)), ((), ())), preferred_element_...]
    pallas_call x0 -> x4, Pallas kernels: none -> 85.1 us  [the longest x1 31.3 us: attention_back(): pl.pallas_call(attend_back_kernel, grid=(packs,), in_specs=[smem, per_pac...]
    ppermute x6 -> x65, starting transfers between devices: 17.9 us -> 92.6 us  [the longest x60 81 us: swap(): return lax.ppermute(value, axis, [(i, i ^ bit) for i in range(peers)])]
    psum x1 -> x0, blocking collectives: 43.8 us -> none  [per_device(): lax.psum((partials[0], partials[1], partials[2], partials[3], partials[4]...]
    ppermute x6 -> x65, waiting for transfers between devices: 72.7 us -> 108 us  [the longest x60 103 us: swap(): return lax.ppermute(value, axis, [(i, i ^ bit) for i in range(peers)])]
    slice x8 -> x5, local copies, waits for them, and re-layouts: 18.6 us -> 1.97 us  [the longest x3 1.35 us: per_device(): gain_one, gain_two = (gain_full[:1], gain_full[1:])]
    unnamed x115 -> x66, local copies, waits for them, and re-layouts: 20.3 us -> 5.14 us
  transfers between devices with their start and end apart: 11 -> 65, of which waited for: 5 -> 25; matrix products, arithmetic and copies ran while one was open for 18% -> 14% of each run, Pallas kernels for 0% -> 17%
where the time goes in v1:
time: 346 us; the launch traced here: 345 us
  waiting for transfers between devices  108 us (31%)
  starting transfers between devices  92.6 us (27%)
  Pallas kernels  85.1 us (25%)
  other arithmetic  20.3 us (6%)
  local copies, waits for them, and re-layouts  19.2 us (6%)
  matrix products  18.5 us (5%)
    ppermute x60, waiting for transfers between devices, swap(): return lax.ppermute(value, axis, [(i, i ^ bit) for i in range(peers)])  103 us
    ppermute x60, starting transfers between devices, swap(): return lax.ppermute(value, axis, [(i, i ^ bit) for i in range(peers)])  81 us
    pallas_call x1, Pallas kernels, attention_back(): pl.pallas_call(attend_back_kernel, grid=(packs,), in_specs=[smem, per_pac...  31.3 us
    pallas_call x1, Pallas kernels, feed_forward(): pl.pallas_call(mlp_kernel, grid=(packs,), in_specs=[smem] + [per_pack(blo...  27.5 us
    pallas_call x1, Pallas kernels, attention_forward(): pl.pallas_call(attend_kernel, grid=(packs,), in_specs=[smem] * 3 + [per_p...  20.3 us
    dot_general x5, matrix products, dot_tn(): lax.dot_general(left, right, (((0,), (0,)), ((), ())), preferred_element_...  18.5 us
    ppermute x5, starting transfers between devices, shifted(): lax.ppermute(value, axis, [(i, i + by) for i in range(peers) if 0 <= i +...  11.5 us
    convert_element_type x12, other arithmetic, added(): return total.astype(BF16)  8.61 us
  transfers between devices with their start and end apart: 65, of which 25 were waited for; matrix products, arithmetic and copies ran while one was open for 14% of the time, Pallas kernels for 17%

profile of v1, /device:TPU:0, one launch (start us, length us, event | category | flops | bytes accessed | tf_op | source)
XLA Modules:
  0.0 345.0 jit_solution(2814762979435982263)
XLA Ops:
  0.7 3.0 collective-permute-start.7
  5.0 18.5 %collective-permute-done.7.s2 = bf16[192,2304]{1,0:T(8,128)(2,1)S(1)} collective-permute-done((bf16[192,2304]{1,0:T(8,128)(2,1)}, bf16[192,2304]{1,0:T(8,128)(2,1)S(1)}, u32[]{:S(2)}, u32[]{:S(2)}) %collective-permute-start.7) | collective-permute-done | bytes 884768 | tf_op jit(solution)/shard_map/ppermute | solution.py:39
  28.6 3.4 collective-permute-done.10.o2
  35.5 3.4 collective-permute-start.1
  40.9 11.3 %collective-permute-done.13.i2 = bf16[192,2304]{1,0:T(8,128)(2,1)} collective-permute-done((bf16[192,2304]{1,0:T(8,128)(2,1)}, bf16[192,2304]{1,0:T(8,128)(2,1)}, u32[]{:S(2)}, u32[]{:S(2)}) %collective-permute-start.13) | collective-permute-done | bytes 884768 | tf_op jit(solution)/shard_map/ppermute | solution.py:39
  57.4 9.2 %collective-permute-done.16.d2 = bf16[288,768]{1,0:T(8,128)(2,1)S(1)} collective-permute-done((bf16[288,768]{1,0:T(8,128)(2,1)}, bf16[288,768]{1,0:T(8,128)(2,1)S(1)}, u32[]{:S(2)}, u32[]{:S(2)}) %collective-permute-start.16) | collective-permute-done | bytes 442400 | tf_op jit(solution)/shard_map/ppermute | solution.py:39
  66.6 20.3 %attend.1 = (bf16[4,256,768]{2,1,0:T(8,128)(2,1)}, bf16[4,384,1536]{2,1,0:T(8,128)(2,1)}, bf16[4,384,768]{2,1,0:T(8,128)(2,1)}, bf16[4,6,2,256,256]{4,3,2,1,0:T(8,128)(2,1)}, bf16[4,256,768]{2,1,0:T(8,128)(2,1)}) custom-call(s32[1]{0:T(128)} %bitcast.me_ref, s32[4]{0:T(128)} %get-tuple-element.90.left_ok, s32[4]{0:T(128)} %get-tuple-element.89.right_ok, ...), custom_call_target="tpu_custom_call" | custom-call | flops 7000000000 | bytes 30000000 | tf_op jit(solution)/shard_map/attend/pallas_call | solution.py:221
  88.3 27.5 %feed_forward.1 = (bf16[4,256,768]{2,1,0:T(8,128)(2,1)}, bf16[4,256,768]{2,1,0:T(8,128)(2,1)}, bf16[4,256,1152]{2,1,0:T(8,128)(2,1)}, bf16[4,256,2304]{2,1,0:T(8...) custom-call(s32[1]{0:T(128)} %bitcast.me_ref, ...), custom_call_target="tpu_custom_call" | custom-call | flops 14000000000 | bytes 40000000 | tf_op jit(solution)/shard_map/feed_forward/pallas_call | solution.py:315
  115.8 3.9 %fusion.2 = bf16[1152,768]{1,0:T(8,128)(2,1)S(1)} fusion(bf16[4,256,1152]{2,1,0:T(8,128)(2,1)} %get-tuple-element.51, bf16[4,256,768]{2,1,0:T(8,128)(2,1)S(1)} %copy-done.13), kind=kOutput, calls=%fused_computation.8 | convolution fusion | flops 1812824064 | bytes 5701632 | tf_op jit(solution)/shard_map/dot_general | solution.py:34
  122.0 4.1 %bitcast_convert_fusion = bf16[768,2304]{1,0:T(8,128)(2,1)S(1)} fusion(bf16[4,256,768]{2,1,0:T(8,128)(2,1)S(1)} %copy-done.31, bf16[4,256,2304]{2,1,0:T(8,128)(2,1)S(1)} %copy-done.27), kind=kOutput, calls=%fused_computation | convolution fusion | flops 3625648128 | bytes 9830400 | tf_op jit(solution)/shard_map/dot_general | solution.py:34
  131.5 31.3 %attend_back.1 = (bf16[4,256,768]{2,1,0:T(8,128)(2,1)}, bf16[4,384,1536]{2,1,0:T(8,128)(2,1)}, f32[4,256,768]{2,1,0:T(8,128)}, bf16[4,64,768]{2,1,0:T(8,128)(2,1...) custom-call(s32[1]{0:T(128)} %bitcast.me_ref, bf16[4,256,768]{2,1,0:T(8,128)(2,1)} %get-tuple-element.35.q_ref, ...), custom_call_target="tpu_custom_call" | custom-call | flops 8999999488 | bytes 30000000 | tf_op jit(solution)/shard_map/attend_back/pallas_call | solution.py:422
  166.6 7.6 %bitcast_convert_fusion.1 = bf16[768,1536]{1,0:T(8,128)(2,1)} fusion(bf16[4,384,768]{2,1,0:T(8,128)(2,1)S(1)} %copy-done.28, bf16[4,384,1536]{2,1,0:T(8,128)(2,1)} %get-tuple-element.47), kind=kOutput, calls=%fused_computation.1 | convolution fusion | flops 3625058304 | bytes 9437184 | tf_op jit(solution)/shard_map/dot_general | solution.py:34
  183.6 2.7 collective-permute-start.24
  190.4 4.3 %collective-permute-start.18 = (bf16[4,64,768]{2,1,0:T(8,128)(2,1)S(1)}, bf16[4,64,768]{2,1,0:T(8,128)(2,1)}, u32[]{:S(2)}, u32[]{:S(2)}) collective-permute-start(bf16[4,64,768]{2,1,0:T(8,128)(2,1)S(1)} %copy-done.23), channel_id=1, source_target_pairs={{0,4},{4,8},{8,12},{12,16},{16,20},{20,24},{24,28},{1,5},{5,9},{9,... | collective-permute-start | bytes 1179656 | tf_op jit(solution)/shard_map/ppermute | solution.py:44
  199.0 5.6 %collective-permute-done.37 = bf16[192,384]{1,0:T(8,128)(2,1)S(1)} collective-permute-done((bf16[192,384]{1,0:T(8,128)(2,1)S(1)}, bf16[192,384]{1,0:T(8,128)(2,1)S(1)}, u32[]{:S(2)}, u32[]{:S(2)}) %collective-permute-start.37) | collective-permute-done | bytes 147488 | tf_op jit(solution)/shard_map/ppermute | solution.py:39
  214.5 3.2 collective-permute-start.41
  218.3 4.4 %collective-permute-done.19.fr_ref = bf16[4,64,768]{2,1,0:T(8,128)(2,1)} collective-permute-done((bf16[4,64,768]{2,1,0:T(8,128)(2,1)S(1)}, bf16[4,64,768]{2,1,0:T(8,128)(2,1)}, u32[]{:S(2)}, u32[]{:S(2)}) %collective-permute-start.19) | collective-permute-done | bytes 393248 | tf_op jit(solution)/shard_map/ppermute | solution.py:44
  222.7 6.0 %finish.1 = bf16[4,256,768]{2,1,0:T(8,128)(2,1)} custom-call(bf16[4,256,768]{2,1,0:T(8,128)(2,1)} %x_ref.7, f32[4,256,768]{2,1,0:T(8,128)} %get-tuple-element.39.own_ref, bf16[4,64,768]{2,1,0:T(8,128)(2,1)} %collective-permute-done.18.fl_ref, bf16[4,64,768]{2,1,0:T(8,128)(2,1)} %collective-permute-done.19.fr_ref, f32[4,256,768]{2,1,0:T(8,128)} %get-tuple-element.42.gm_ref, ...), custom_call_target="tpu_custom_call" | custom-call | flops 20000000 | bytes 10000000 | tf_op jit(solution)/shard_map/finish/pallas_call | solution.py:482
  236.8 4.3 %collective-permute-done.57 = bf16[288,384]{1,0:T(8,128)(2,1)S(1)} collective-permute-done((bf16[288,384]{1,0:T(8,128)(2,1)S(1)}, bf16[288,384]{1,0:T(8,128)(2,1)S(1)}, u32[]{:S(2)}, u32[]{:S(2)}) %collective-permute-start.57) | collective-permute-done | bytes 221216 | tf_op jit(solution)/shard_map/ppermute | solution.py:39
  246.8 2.5 collective-permute-done.60
  250.3 3.2 collective-permute-start.62
  255.7 3.8 %collective-permute-done.63 = bf16[72,384]{1,0:T(8,128)(2,1)S(1)} collective-permute-done((bf16[72,384]{1,0:T(8,128)(2,1)S(1)}, bf16[72,384]{1,0:T(8,128)(2,1)S(1)}, u32[]{:S(2)}, u32[]{:S(2)}) %collective-permute-start.63) | collective-permute-done | bytes 55328 | tf_op jit(solution)/shard_map/ppermute | solution.py:39
  267.0 17.5 %collective-permute-done.46 = bf16[192,2304]{1,0:T(8,128)(2,1)S(1)} collective-permute-done((bf16[192,2304]{1,0:T(8,128)(2,1)S(1)}, bf16[192,2304]{1,0:T(8,128)(2,1)S(1)}, u32[]{:S(2)}, u32[]{:S(2)}) %collective-permute-start.46) | collective-permute-done | bytes 884768 | tf_op jit(solution)/shard_map/ppermute | solution.py:39
  286.6 7.7 %collective-permute-done.26 = bf16[192,2304]{1,0:T(8,128)(2,1)S(1)} collective-permute-done((bf16[192,2304]{1,0:T(8,128)(2,1)S(1)}, bf16[192,2304]{1,0:T(8,128)(2,1)S(1)}, u32[]{:S(2)}, u32[]{:S(2)}) %collective-permute-start.26) | collective-permute-done | bytes 884768 | tf_op jit(solution)/shard_map/ppermute | solution.py:39
  299.5 2.8 collective-permute-start.50
  303.2 2.9 collective-permute-start.29
  307.6 2.6 collective-permute-done.49
  310.4 7.1 %collective-permute-start.51 = (bf16[48,1152]{1,0:T(8,128)(2,1)S(1)}, bf16[48,1152]{1,0:T(8,128)(2,1)S(1)}, u32[]{:S(2)}, u32[]{:S(2)}) collective-permute-start(bf16[48,1152]{1,0:T(8,128)(2,1)S(1)} %get-tuple-element.55), channel_id=1, source_target_pairs={{0,8},{4,12},{8,0},{12,4},{16,24},{20,28},{24,16},{28,20},{1,9},{5... | collective-permute-start | bytes 331784 | tf_op jit(solution)/shard_map/ppermute | solution.py:39
  317.5 2.4 collective-permute-start.53
  320.1 6.9 %collective-permute-start.31 = (bf16[48,1152]{1,0:T(8,128)(2,1)S(1)}, bf16[48,1152]{1,0:T(8,128)(2,1)S(1)}, u32[]{:S(2)}, u32[]{:S(2)}) collective-permute-start(bf16[48,1152]{1,0:T(8,128)(2,1)S(1)} %get-tuple-element.59), channel_id=1, source_target_pairs={{0,8},{4,12},{8,0},{12,4},{16,24},{20,28},{24,16},{28,20},{1,9},{5... | collective-permute-start | bytes 331784 | tf_op jit(solution)/shard_map/ppermute | solution.py:39
  331.3 3.4 collective-permute-done.32
  340.2 3.3 collective-permute-done.34
  (263 shorter events, 103.2 us)
Async XLA Ops:
  0.7 22.9 %collective-permute-start.7 = (bf16[192,2304]{1,0:T(8,128)(2,1)}, bf16[192,2304]{1,0:T(8,128)(2,1)S(1)}, u32[]{:S(2)}, u32[]{:S(2)}) collective-permute-start(bf16[192,2304]{1,0:T(8,128)(2,1)} %s0.3), channel_id=1, source_target_pairs={{0,2},{1,3},{2,0},{3,1},{4,6},{5,7},{6,4},{7,5},{8,10},{9,11},{10,... | collective-permute-start | bytes 2654216 | tf_op jit(solution)/shard_map/ppermute | solution.py:39
  25.3 13.6 %collective-permute-start.3 = (bf16[2,192]{1,0:T(2,128)(2,1)S(1)}, bf16[2,192]{1,0:T(2,128)(2,1)S(1)}, u32[]{:S(2)}, u32[]{:S(2)}) collective-permute-start(bf16[2,192]{1,0:T(2,128)(2,1)S(1)} %pad_maximum_fusion.4), channel_id=1, source_target_pairs={{0,1},{1,0},{2,3},{3,2},{4,5},{5,4},{6,7},{7,6},{8,9},{9,8},{10,11... | collective-permute-start | bytes 2312 | tf_op jit(solution)/shard_map/ppermute | solution.py:39
  25.4 14.8 %collective-permute-start.4 = (bf16[2,192]{1,0:T(2,128)(2,1)S(1)}, bf16[2,192]{1,0:T(2,128)(2,1)S(1)}, u32[]{:S(2)}, u32[]{:S(2)}) collective-permute-start(bf16[2,192]{1,0:T(2,128)(2,1)S(1)} %pad_maximum_fusion.4), channel_id=1, source_target_pairs={{0,2},{1,3},{2,0},{3,1},{4,6},{5,7},{6,4},{7,5},{8,10},{9,11},{10,... | collective-permute-start | bytes 2312 | tf_op jit(solution)/shard_map/ppermute | solution.py:39
  25.7 29.3 %collective-permute-start.6 = (bf16[192,2304]{1,0:T(8,128)(2,1)}, bf16[192,2304]{1,0:T(8,128)(2,1)}, u32[]{:S(2)}, u32[]{:S(2)}) collective-permute-start(bf16[192,2304]{1,0:T(8,128)(2,1)} %s0.3), channel_id=1, source_target_pairs={{0,1},{1,0},{2,3},{3,2},{4,5},{5,4},{6,7},{7,6},{8,9},{9,8},{10,11... | collective-permute-start | bytes 2654216 | tf_op jit(solution)/shard_map/ppermute | solution.py:39
  32.0 20.2 %collective-permute-start.13 = (bf16[192,2304]{1,0:T(8,128)(2,1)}, bf16[192,2304]{1,0:T(8,128)(2,1)}, u32[]{:S(2)}, u32[]{:S(2)}) collective-permute-start(bf16[192,2304]{1,0:T(8,128)(2,1)} %i0), channel_id=1, source_target_pairs={{0,2},{1,3},{2,0},{3,1},{4,6},{5,7},{6,4},{7,5},{8,10},{9,11},{10,... | collective-permute-start | bytes 2654216 | tf_op jit(solution)/shard_map/ppermute | solution.py:39
  35.5 18.3 %collective-permute-start.1 = (bf16[4,64,768]{2,1,0:T(8,128)(2,1)S(1)}, bf16[4,64,768]{2,1,0:T(8,128)(2,1)S(1)}, u32[]{:S(2)}, u32[]{:S(2)}) collective-permute-start(bf16[4,64,768]{2,1,0:T(8,128)(2,1)S(1)} %get-tuple-element.61), channel_id=1, source_target_pairs={{0,4},{4,8},{8,12},{12,16},{16,20},{20,24},{24,28},{1,5},{5,9},{9,... | collective-permute-start | bytes 1179656 | tf_op jit(solution)/shard_map/ppermute | solution.py:44
  38.9 15.0 %collective-permute-start.2 = (bf16[4,64,768]{2,1,0:T(8,128)(2,1)S(1)}, bf16[4,64,768]{2,1,0:T(8,128)(2,1)S(1)}, u32[]{:S(2)}, u32[]{:S(2)}) collective-permute-start(bf16[4,64,768]{2,1,0:T(8,128)(2,1)S(1)} %get-tuple-element.60), channel_id=1, source_target_pairs={{4,0},{8,4},{12,8},{16,12},{20,16},{24,20},{28,24},{5,1},{9,5},{13... | collective-permute-start | bytes 1179656 | tf_op jit(solution)/shard_map/ppermute | solution.py:44
  40.2 17.1 %collective-permute-start.8 = (bf16[192,2304]{1,0:T(8,128)(2,1)}, bf16[192,2304]{1,0:T(8,128)(2,1)S(1)}, u32[]{:S(2)}, u32[]{:S(2)}) collective-permute-start(bf16[192,2304]{1,0:T(8,128)(2,1)} %copy-done.15), channel_id=1, source_target_pairs={{0,1},{1,0},{2,3},{3,2},{4,5},{5,4},{6,7},{7,6},{8,9},{9,8},{10,11... | collective-permute-start | bytes 2654216 | tf_op jit(solution)/shard_map/ppermute | solution.py:39
  53.8 33.2 %collective-permute-start.12 = (bf16[192,2304]{1,0:T(8,128)(2,1)S(1)}, bf16[192,2304]{1,0:T(8,128)(2,1)}, u32[]{:S(2)}, u32[]{:S(2)}) collective-permute-start(bf16[192,2304]{1,0:T(8,128)(2,1)S(1)} %copy-done.14), channel_id=1, source_target_pairs={{0,1},{1,0},{2,3},{3,2},{4,5},{5,4},{6,7},{7,6},{8,9},{9,8},{10,11... | collective-permute-start | bytes 2654216 | tf_op jit(solution)/shard_map/ppermute | solution.py:39
  53.9 12.6 %collective-permute-start.16 = (bf16[288,768]{1,0:T(8,128)(2,1)}, bf16[288,768]{1,0:T(8,128)(2,1)S(1)}, u32[]{:S(2)}, u32[]{:S(2)}) collective-permute-start(bf16[288,768]{1,0:T(8,128)(2,1)} %d0), channel_id=1, source_target_pairs={{0,2},{1,3},{2,0},{3,1},{4,6},{5,7},{6,4},{7,5},{8,10},{9,11},{10,... | collective-permute-start | bytes 1327112 | tf_op jit(solution)/shard_map/ppermute | solution.py:39
  55.0 32.0 %collective-permute-start.14 = (bf16[192,2304]{1,0:T(8,128)(2,1)}, bf16[192,2304]{1,0:T(8,128)(2,1)S(1)}, u32[]{:S(2)}, u32[]{:S(2)}) collective-permute-start(bf16[192,2304]{1,0:T(8,128)(2,1)} %collective-permute-done.13.i2), channel_id=1, source_target_pairs={{0,1},{1,0},{2,3},{3,2},{4,5},{5,4},{6,7},{7,6},{8,9},{9,8},{10,11... | collective-permute-start | bytes 2654216 | tf_op jit(solution)/shard_map/ppermute | solution.py:39
  56.8 30.1 %collective-permute-start.11 = (bf16[192,768]{1,0:T(8,128)(2,1)}, bf16[192,768]{1,0:T(8,128)(2,1)S(1)}, u32[]{:S(2)}, u32[]{:S(2)}) collective-permute-start(bf16[192,768]{1,0:T(8,128)(2,1)} %copy-done.25), channel_id=1, source_target_pairs={{0,1},{1,0},{2,3},{3,2},{4,5},{5,4},{6,7},{7,6},{8,9},{9,8},{10,11... | collective-permute-start | bytes 884744 | tf_op jit(solution)/shard_map/ppermute | solution.py:39
  57.3 29.7 %collective-permute-start.15 = (bf16[288,768]{1,0:T(8,128)(2,1)}, bf16[288,768]{1,0:T(8,128)(2,1)S(1)}, u32[]{:S(2)}, u32[]{:S(2)}) collective-permute-start(bf16[288,768]{1,0:T(8,128)(2,1)} %d0), channel_id=1, source_target_pairs={{0,1},{1,0},{2,3},{3,2},{4,5},{5,4},{6,7},{7,6},{8,9},{9,8},{10,11... | collective-permute-start | bytes 1327112 | tf_op jit(solution)/shard_map/ppermute | solution.py:39
  66.6 20.4 %collective-permute-start.17 = (bf16[288,768]{1,0:T(8,128)(2,1)S(1)}, bf16[288,768]{1,0:T(8,128)(2,1)S(1)}, u32[]{:S(2)}, u32[]{:S(2)}) collective-permute-start(bf16[288,768]{1,0:T(8,128)(2,1)S(1)} %collective-permute-done.16.d2), channel_id=1, source_target_pairs={{0,1},{1,0},{2,3},{3,2},{4,5},{5,4},{6,7},{7,6},{8,9},{9,8},{10,11... | collective-permute-start | bytes 1327112 | tf_op jit(solution)/shard_map/ppermute | solution.py:39
  120.6 76.9 %collective-permute-start.55 = (bf16[2,288,768]{2,1,0:T(8,128)(2,1)}, bf16[2,288,768]{2,1,0:T(8,128)(2,1)}, u32[]{:S(2)}, u32[]{:S(2)}) collective-permute-start(bf16[2,288,768]{2,1,0:T(8,128)(2,1)} %dynamic-slice_bitcast_fusion.2), channel_id=1, source_target_pairs={{0,1},{1,0},{2,3},{3,2},{4,5},{5,4},{6,7},{7,6},{8,9},{9,8},{10,11... | collective-permute-start | bytes 2654216 | tf_op jit(solution)/shard_map/ppermute | solution.py:39
  128.8 131.0 %collective-permute-start.45 = (bf16[2,192,2304]{2,1,0:T(8,128)(2,1)}, bf16[2,192,2304]{2,1,0:T(8,128)(2,1)}, u32[]{:S(2)}, u32[]{:S(2)}) collective-permute-start(bf16[2,192,2304]{2,1,0:T(8,128)(2,1)} %dynamic-slice_bitcast_fusion), channel_id=1, source_target_pairs={{0,1},{1,0},{2,3},{3,2},{4,5},{5,4},{6,7},{7,6},{8,9},{9,8},{10,11... | collective-permute-start | bytes 5308424 | tf_op jit(solution)/shard_map/ppermute | solution.py:39
  164.8 21.5 %collective-permute-start.35 = (bf16[2,192,768]{2,1,0:T(8,128)(2,1)}, bf16[2,192,768]{2,1,0:T(8,128)(2,1)}, u32[]{:S(2)}, u32[]{:S(2)}) collective-permute-start(bf16[2,192,768]{2,1,0:T(8,128)(2,1)} %dynamic-slice_bitcast_fusion.5), channel_id=1, source_target_pairs={{0,1},{1,0},{2,3},{3,2},{4,5},{5,4},{6,7},{7,6},{8,9},{9,8},{10,11... | collective-permute-start | bytes 1769480 | tf_op jit(solution)/shard_map/ppermute | solution.py:39
  190.4 27.8 %collective-permute-start.18 = (bf16[4,64,768]{2,1,0:T(8,128)(2,1)S(1)}, bf16[4,64,768]{2,1,0:T(8,128)(2,1)}, u32[]{:S(2)}, u32[]{:S(2)}) collective-permute-start(bf16[4,64,768]{2,1,0:T(8,128)(2,1)S(1)} %copy-done.23), channel_id=1, source_target_pairs={{0,4},{4,8},{8,12},{12,16},{16,20},{20,24},{24,28},{1,5},{5,9},{9,... | collective-permute-start | bytes 1179656 | tf_op jit(solution)/shard_map/ppermute | solution.py:44
  210.2 12.5 %collective-permute-start.19 = (bf16[4,64,768]{2,1,0:T(8,128)(2,1)S(1)}, bf16[4,64,768]{2,1,0:T(8,128)(2,1)}, u32[]{:S(2)}, u32[]{:S(2)}) collective-permute-start(bf16[4,64,768]{2,1,0:T(8,128)(2,1)S(1)} %copy-done.21), channel_id=1, source_target_pairs={{4,0},{8,4},{12,8},{16,12},{20,16},{24,20},{28,24},{5,1},{9,5},{13... | collective-permute-start | bytes 1179656 | tf_op jit(solution)/shard_map/ppermute | solution.py:44
  212.4 20.7 %collective-permute-start.56 = (bf16[288,768]{1,0:T(8,128)(2,1)}, bf16[288,768]{1,0:T(8,128)(2,1)}, u32[]{:S(2)}, u32[]{:S(2)}) collective-permute-start(bf16[288,768]{1,0:T(8,128)(2,1)} %dynamic-slice_bitcast_fusion.6), channel_id=1, source_target_pairs={{0,2},{1,3},{2,0},{3,1},{4,6},{5,7},{6,4},{7,5},{8,10},{9,11},{10,... | collective-permute-start | bytes 1327112 | tf_op jit(solution)/shard_map/ppermute | solution.py:39
  214.5 14.9 %collective-permute-start.41 = (bf16[48,384]{1,0:T(8,128)(2,1)}, bf16[48,384]{1,0:T(8,128)(2,1)}, u32[]{:S(2)}, u32[]{:S(2)}) collective-permute-start(bf16[48,384]{1,0:T(8,128)(2,1)} %get-tuple-element.57), channel_id=1, source_target_pairs={{0,8},{4,12},{8,0},{12,4},{16,24},{20,28},{24,16},{28,20},{1,9},{5... | collective-permute-start | bytes 110600 | tf_op jit(solution)/shard_map/ppermute | solution.py:39
  218.3 44.2 %collective-permute-start.25 = (bf16[2,192,2304]{2,1,0:T(8,128)(2,1)}, bf16[2,192,2304]{2,1,0:T(8,128)(2,1)}, u32[]{:S(2)}, u32[]{:S(2)}) collective-permute-start(bf16[2,192,2304]{2,1,0:T(8,128)(2,1)} %dynamic-slice_bitcast_fusion.1), channel_id=1, source_target_pairs={{0,1},{1,0},{2,3},{3,2},{4,5},{5,4},{6,7},{7,6},{8,9},{9,8},{10,11... | collective-permute-start | bytes 5308424 | tf_op jit(solution)/shard_map/ppermute | solution.py:39
  261.9 22.7 %collective-permute-start.46 = (bf16[192,2304]{1,0:T(8,128)(2,1)S(1)}, bf16[192,2304]{1,0:T(8,128)(2,1)S(1)}, u32[]{:S(2)}, u32[]{:S(2)}) collective-permute-start(bf16[192,2304]{1,0:T(8,128)(2,1)S(1)} %dynamic-slice_bitcast_fusion.3), channel_id=1, source_target_pairs={{0,2},{1,3},{2,0},{3,1},{4,6},{5,7},{6,4},{7,5},{8,10},{9,11},{10,... | collective-permute-start | bytes 2654216 | tf_op jit(solution)/shard_map/ppermute | solution.py:39
  264.4 29.9 %collective-permute-start.26 = (bf16[192,2304]{1,0:T(8,128)(2,1)S(1)}, bf16[192,2304]{1,0:T(8,128)(2,1)S(1)}, u32[]{:S(2)}, u32[]{:S(2)}) collective-permute-start(bf16[192,2304]{1,0:T(8,128)(2,1)S(1)} %dynamic-slice_bitcast_fusion.4), channel_id=1, source_target_pairs={{0,2},{1,3},{2,0},{3,1},{4,6},{5,7},{6,4},{7,5},{8,10},{9,11},{10,... | collective-permute-start | bytes 2654216 | tf_op jit(solution)/shard_map/ppermute | solution.py:39
  284.8 12.9 %collective-permute-start.47 = (bf16[192,1152]{1,0:T(8,128)(2,1)S(1)}, bf16[192,1152]{1,0:T(8,128)(2,1)S(1)}, u32[]{:S(2)}, u32[]{:S(2)}) collective-permute-start(bf16[192,1152]{1,0:T(8,128)(2,1)S(1)} %constant_dynamic-slice_fusion.8), channel_id=1, source_target_pairs={{0,4},{4,0},{8,12},{12,8},{16,20},{20,16},{24,28},{28,24},{1,5},{5... | collective-permute-start | bytes 1327112 | tf_op jit(solution)/shard_map/ppermute | solution.py:39
  298.0 12.3 %collective-permute-start.49 = (bf16[48,1152]{1,0:T(8,128)(2,1)S(1)}, bf16[48,1152]{1,0:T(8,128)(2,1)S(1)}, u32[]{:S(2)}, u32[]{:S(2)}) collective-permute-start(bf16[48,1152]{1,0:T(8,128)(2,1)S(1)} %get-tuple-element.70), channel_id=1, source_target_pairs={{0,16},{4,20},{8,24},{12,28},{16,0},{20,4},{24,8},{28,12},{1,17},{... | collective-permute-start | bytes 331784 | tf_op jit(solution)/shard_map/ppermute | solution.py:39
  303.1 14.4 %collective-permute-start.28 = (bf16[48,1152]{1,0:T(8,128)(2,1)S(1)}, bf16[48,1152]{1,0:T(8,128)(2,1)S(1)}, u32[]{:S(2)}, u32[]{:S(2)}) collective-permute-start(bf16[48,1152]{1,0:T(8,128)(2,1)S(1)} %get-tuple-element.71), channel_id=1, source_target_pairs={{0,8},{4,12},{8,0},{12,4},{16,24},{20,28},{24,16},{28,20},{1,9},{5... | collective-permute-start | bytes 331784 | tf_op jit(solution)/shard_map/ppermute | solution.py:39
  303.2 16.7 %collective-permute-start.29 = (bf16[48,1152]{1,0:T(8,128)(2,1)S(1)}, bf16[48,1152]{1,0:T(8,128)(2,1)S(1)}, u32[]{:S(2)}, u32[]{:S(2)}) collective-permute-start(bf16[48,1152]{1,0:T(8,128)(2,1)S(1)} %get-tuple-element.73), channel_id=1, source_target_pairs={{0,16},{4,20},{8,24},{12,28},{16,0},{20,4},{24,8},{28,12},{1,17},{... | collective-permute-start | bytes 331784 | tf_op jit(solution)/shard_map/ppermute | solution.py:39
  306.1 13.9 %collective-permute-start.30 = (bf16[48,1152]{1,0:T(8,128)(2,1)S(1)}, bf16[48,1152]{1,0:T(8,128)(2,1)S(1)}, u32[]{:S(2)}, u32[]{:S(2)}) collective-permute-start(bf16[48,1152]{1,0:T(8,128)(2,1)S(1)} %get-tuple-element.72), channel_id=1, source_target_pairs={{0,24},{4,28},{8,16},{12,20},{16,8},{20,12},{24,0},{28,4},{1,25},{... | collective-permute-start | bytes 331784 | tf_op jit(solution)/shard_map/ppermute | solution.py:39
  310.4 16.6 %collective-permute-start.51 = (bf16[48,1152]{1,0:T(8,128)(2,1)S(1)}, bf16[48,1152]{1,0:T(8,128)(2,1)S(1)}, u32[]{:S(2)}, u32[]{:S(2)}) collective-permute-start(bf16[48,1152]{1,0:T(8,128)(2,1)S(1)} %get-tuple-element.55), channel_id=1, source_target_pairs={{0,8},{4,12},{8,0},{12,4},{16,24},{20,28},{24,16},{28,20},{1,9},{5... | collective-permute-start | bytes 331784 | tf_op jit(solution)/shard_map/ppermute | solution.py:39
  317.5 11.9 %collective-permute-start.52 = (bf16[48,1152]{1,0:T(8,128)(2,1)S(1)}, bf16[48,1152]{1,0:T(8,128)(2,1)S(1)}, u32[]{:S(2)}, u32[]{:S(2)}) collective-permute-start(bf16[48,1152]{1,0:T(8,128)(2,1)S(1)} %get-tuple-element.55), channel_id=1, source_target_pairs={{0,16},{4,20},{8,24},{12,28},{16,0},{20,4},{24,8},{28,12},{1,17},{... | collective-permute-start | bytes 331784 | tf_op jit(solution)/shard_map/ppermute | solution.py:39
  317.5 12.0 %collective-permute-start.53 = (bf16[48,1152]{1,0:T(8,128)(2,1)S(1)}, bf16[48,1152]{1,0:T(8,128)(2,1)S(1)}, u32[]{:S(2)}, u32[]{:S(2)}) collective-permute-start(bf16[48,1152]{1,0:T(8,128)(2,1)S(1)} %get-tuple-element.55), channel_id=1, source_target_pairs={{0,24},{4,28},{8,16},{12,20},{16,8},{20,12},{24,0},{28,4},{1,25},{... | collective-permute-start | bytes 331784 | tf_op jit(solution)/shard_map/ppermute | solution.py:39
  (66 other events, 624.1 us)
